TPU v7x, 128 devices: a whole 4x4x4 slice. The times are simulated.
128 devices in a mesh: gx: 2 (over z_lo), gy: 4 (over x), mem: 16 (over z_hi, y, core).
Axes of the slice: x: 4, y: 4, z: 4 (z_hi: 2, z_lo: 2; z = z_hi * 2 + z_lo), core: 2. Of those that a mesh axis runs over, the one named last changes fastest.
Arguments:
- prior_members: float32 [8, 512, 128, 512], P(None, 'mem', 'gx', 'gy'), may hold values from -30 to 30
- courant_x: float32 [128, 512], P('gx', 'gy'), may hold values from -0.4 to 0.4
- courant_y: float32 [128, 512], P('gx', 'gy'), may hold values from -0.4 to 0.4
- diffusion: float32 [128, 512], P('gx', 'gy'), may hold values from 0.01 to 0.05
- report_level: int32 [32, 4, 256], P('gx', 'gy'), may hold values from 0 to 3
- report_cell: int32 [32, 4, 256], P('gx', 'gy'), may hold values from 0 to 511
- report_value: float32 [32, 4, 256], P('gx', 'gy'), may hold values from -6 to 6
- report_precision: float32 [32, 4, 256], P('gx', 'gy'), may hold values from 0.5 to 4
- report_class: int32 [32, 4, 256], P('gx', 'gy'), may hold values from 0 to 7
- report_count: int32 [32, 4], P('gx', 'gy'), may hold values from 64 to 256, as said below
Outputs:
- analysis: float32 [8, 512, 128, 512], P(None, 'mem', 'gx', 'gy')
Inputs may be any that keep to these rules, and one draw needn't show every extreme that they name: A tile uses observation slots 0 to report_count - 1; some tile uses all 256.
All inputs are finite; a program needn't handle non-finite values.
Results may differ from a plain program's by a relative error of at most 0.0003.
Values sent between devices are 32-bit elements; how exact they have to be, the bound alone decides.
No kernel may reach another device: no remote copies, remote signals or barrier semaphores. Data moves between devices by JAX's collectives and lax.ppermute only.
A program may use at most 192 MiB of HBM per device.

v0:
```python
import jax
import jax.numpy as jnp
from jax import lax
from jax.sharding import PartitionSpec as P

TILES_DEV = 1
STEPS = 2
NEWTON = 8


def with_halo(cells, sides, width):
    for axis, dim in sides:
        count = lax.axis_size(axis)
        head = lax.slice_in_dim(cells, 0, width, axis=dim)
        tail = lax.slice_in_dim(cells, cells.shape[dim] - width, cells.shape[dim], axis=dim)
        cells = jnp.concatenate(
            [
                lax.ppermute(tail, axis, [(i, (i + 1) % count) for i in range(count)]),
                cells,
                lax.ppermute(head, axis, [((i + 1) % count, i) for i in range(count)]),
            ],
            axis=dim,
        )
    return cells


def update(centre, western, eastern, southern, northern, plus_x, minus_x, plus_y, minus_y, spread):
    moved = centre - plus_x * (centre - western) - minus_x * (eastern - centre)
    moved = moved - plus_y * (centre - southern) - minus_y * (northern - centre)
    return moved + spread * (eastern + western + northern + southern - 4.0 * centre)


def advance_padded(padded, coefficients):
    centre = padded[:, 1:-1, 1:-1]
    western = padded[:, :-2, 1:-1]
    eastern = padded[:, 2:, 1:-1]
    southern = padded[:, 1:-1, :-2]
    northern = padded[:, 1:-1, 2:]
    plus_x = jnp.maximum(coefficients[0], 0.0)
    minus_x = jnp.minimum(coefficients[0], 0.0)
    plus_y = jnp.maximum(coefficients[1], 0.0)
    minus_y = jnp.minimum(coefficients[1], 0.0)
    return update(
        centre,
        western,
        eastern,
        southern,
        northern,
        plus_x,
        minus_x,
        plus_y,
        minus_y,
        coefficients[2],
    )


def mixing_matrix(raw_values, report_value, report_precision, report_class, slot_count):
    members = raw_values.shape[0]
    slots = raw_values.shape[1]
    centre_obs = jnp.sum(raw_values, axis=0) / members
    observed = raw_values - centre_obs
    innovation = report_value - centre_obs
    usable = (jnp.arange(slots) < slot_count).astype(jnp.float32)
    weight = usable * report_precision / (1.0 + report_class.astype(jnp.float32))
    identity = jnp.eye(members, dtype=jnp.float32)
    gram_matrix = (
        jnp.dot(observed * weight, observed.T, precision=lax.Precision.HIGHEST)
        + (members - 1.0) * identity
    )
    norm_scale = jnp.sqrt(jnp.sum(gram_matrix * gram_matrix))
    root_y = gram_matrix / norm_scale
    root_z = identity
    for iteration in range(NEWTON):
        factor = 1.5 * identity - 0.5 * jnp.dot(root_z, root_y, precision=lax.Precision.HIGHEST)
        new_z = jnp.dot(factor, root_z, precision=lax.Precision.HIGHEST)
        if iteration + 1 < NEWTON:
            root_y = jnp.dot(root_y, factor, precision=lax.Precision.HIGHEST)
        root_z = new_z
    driven = jnp.dot(observed, weight * innovation, precision=lax.Precision.HIGHEST)
    mean_shift = (
        jnp.dot(
            root_z,
            jnp.dot(root_z, driven, precision=lax.Precision.HIGHEST),
            precision=lax.Precision.HIGHEST,
        )
        / norm_scale
    )
    return jnp.sqrt((members - 1.0) / norm_scale) * root_z + mean_shift[:, None]


def transform(taper_patch, mixing):
    members = taper_patch.shape[1]
    centre = jnp.sum(taper_patch, axis=1, keepdims=True) / members
    anomaly = taper_patch - centre
    return centre + jnp.einsum("fjc,jk->fkc", anomaly, mixing, precision=lax.Precision.HIGHEST)


def own_rows(table, first_tile, tiles_dev):
    flat_table = table.reshape((table.shape[0] * table.shape[1],) + table.shape[2:])
    return lax.dynamic_slice_in_dim(flat_table, first_tile, tiles_dev, 0)


def on_device(
    prior_members,
    courant_x,
    courant_y,
    diffusion,
    report_level,
    report_cell,
    report_value,
    report_precision,
    report_class,
    report_count,
):
    fields_all, members_dev, cells_x, cells_y = prior_members.shape
    stacked_fields = prior_members.reshape(fields_all * members_dev, cells_x, cells_y)
    coefficients = jnp.stack([courant_x, courant_y, diffusion])
    for number in range(STEPS):
        padded = with_halo(stacked_fields, (("gx", 1), ("gy", 2)), 1)
        stacked_fields = advance_padded(padded, coefficients)
    stepped = stacked_fields.reshape(fields_all, members_dev, cells_x * cells_y)
    tiles_dev = TILES_DEV
    first_tile = lax.axis_index("mem") * tiles_dev
    own_level = own_rows(report_level, first_tile, tiles_dev)
    own_cell = own_rows(report_cell, first_tile, tiles_dev)
    own_value = own_rows(report_value, first_tile, tiles_dev)
    own_precision = own_rows(report_precision, first_tile, tiles_dev)
    own_class = own_rows(report_class, first_tile, tiles_dev)
    own_count = own_rows(report_count, first_tile, tiles_dev)
    groups = [lax.all_to_all(stepped, "mem", split_axis=2, concat_axis=1, tiled=True)]
    results = [[] for group_block in groups]
    raw_values = groups[0][own_level[0], :, 0 + own_cell[0]].T
    mixing = mixing_matrix(raw_values, own_value[0], own_precision[0], own_class[0], own_count[0])
    results[0].append(transform(groups[0], mixing))
    analysed = jnp.concatenate([pieces[0] for pieces in results], axis=0)
    returned = lax.all_to_all(analysed, "mem", split_axis=1, concat_axis=2, tiled=True)
    return returned.reshape(fields_all, members_dev, cells_x, cells_y)


def solution(mesh):
    in_specs = (
        P(None, "mem", "gx", "gy"),
        P("gx", "gy"),
        P("gx", "gy"),
        P("gx", "gy"),
        P("gx", "gy", None),
        P("gx", "gy", None),
        P("gx", "gy", None),
        P("gx", "gy", None),
        P("gx", "gy", None),
        P("gx", "gy"),
    )
    out_specs = P(None, "mem", "gx", "gy")
    return jax.shard_map(
        on_device, mesh=mesh, in_specs=in_specs, out_specs=out_specs, check_vma=False
    )
```

profile of v0, /device:TPU:6, one launch (start us, length us, event | category | flops | bytes accessed | tf_op | source)
XLA Modules:
  0.0 623.0 jit_solution(13925740101798682754)
XLA Ops:
  1.8 2.0 collective-permute-start.1
  3.9 4.3 collective-permute-done.1
  8.2 1.9 collective-permute-done
  10.1 4.1 pad_maximum_fusion
  14.1 7.9 %fusion.53 = (f32[256,66,1]{2,1,0:T(8,128)}, f32[256,66,1]{2,1,0:T(8,128)}) fusion(f32[256,66,128]{2,1,0:T(8,128)S(1)} %pad_maximum_fusion), kind=kLoop, calls=%fused_computation.112 | loop fusion | bytes 270336 | tf_op jit(solution)/shard_map/slice | solution.py:15
  22.0 6.1 copy.46
  29.0 6.1 copy.44
  35.1 2.5 collective-permute-start.2
  37.6 5.7 copy.47
  43.3 5.7 copy.45
  49.0 25.4 %fusion.20 = f32[256,64,128]{2,1,0:T(8,128)S(1)} fusion(f32[256,1,128]{2,1,0:T(1,128)S(1)} %collective-permute-done.1, f32[256,64,128]{2,1,0:T(8,128)} %bitcast.103, f32[256,1,128]{2,1,0:T(1,128)S(1)} %collective-permute-done, f32[256,66,1]{2,1,0:T(8,128)} %copy.47, f32[256,66,1]{2,1,0:T(8,128)} %copy.45, f32[64,128]{1,0:T(8,128)S(1)} %copy-done.13, ...), kind=kLoop, calls=%fused_computation.38 | loop fusion | flops 56623104 | bytes 17338368 | tf_op jit(solution)/shard_map/add | solution.py:30
  77.0 3.2 collective-permute-done.5
  81.8 2.3 pad_maximum_fusion.1
  84.1 7.9 %fusion.52 = (f32[256,66,1]{2,1,0:T(8,128)}, f32[256,66,1]{2,1,0:T(8,128)}) fusion(f32[256,66,128]{2,1,0:T(8,128)S(1)} %pad_maximum_fusion.1), kind=kLoop, calls=%fused_computation.111 | loop fusion | bytes 270336 | tf_op jit(solution)/shard_map/slice | solution.py:15
  92.0 6.1 copy.50
  98.2 6.1 copy.48
  104.3 3.3 collective-permute-start.6
  107.6 5.7 copy.51
  113.3 5.7 copy.49
  119.0 27.2 %fusion.6 = f32[256,64,128]{2,1,0:T(8,128)} fusion(f32[256,1,128]{2,1,0:T(1,128)S(1)} %copy-done.4, f32[256,64,128]{2,1,0:T(8,128)} %copy-done.2, f32[256,1,128]{2,1,0:T(1,128)} %collective-permute-done.4, f32[256,66,1]{2,1,0:T(8,128)} %copy.51, f32[256,66,1]{2,1,0:T(8,128)} %copy.49, f32[64,128]{1,0:T(8,128)S(1)} %copy-done.14, f32[64,128]{1,0:T(8,128)S(1)} %copy-done.8, ...), kind=kLoop, calls=%fused_computation.16 | loop fusion | flops 56623104 | bytes 17338368 | tf_op jit(solution)/shard_map/add | solution.py:30
  146.3 9.4 %reshape.117 = f32[8,32,8192]{2,1,0:T(8,128)} reshape(f32[256,64,128]{2,1,0:T(8,128)} %fusion.6) | data formatting | bytes 16777216 | tf_op jit(solution)/shard_map/reshape | solution.py:121
  155.6 19.8 %copy.52 = f32[8,32,8192]{1,0,2:T(8,128)} copy(f32[8,32,8192]{2,1,0:T(8,128)} %reshape.117) | data formatting | bytes 16777216 | tf_op jit(solution)/shard_map/reshape | solution.py:121
  175.4 24.2 %reshape.132 = f32[16,1,131072]{2,1,0:T(1,128)} reshape(f32[8192,8,32]{2,1,0:T(8,128)} %bitcast.100) | data formatting | bytes 16777216
  199.6 8.1 %all-to-all-start = ((f32[16,1,131072]{2,1,0:T(1,128)}), f32[16,1,131072]{2,1,0:T(1,128)}, u32[]{:S(2)}, u32[]{:S(2)}) async-start(f32[16,1,131072]{2,1,0:T(1,128)} %reshape.132), calls=%async_computation | async-start | bytes 16777216 | tf_op jit(solution)/shard_map/all_to_all | solution.py:130
  210.4 110.3 %all-to-all-done = f32[16,1,131072]{2,1,0:T(1,128)} async-done(((f32[16,1,131072]{2,1,0:T(1,128)}), f32[16,1,131072]{2,1,0:T(1,128)}, u32[]{:S(2)}, u32[]{:S(2)}) %all-to-all-start) | async-done | bytes 8388640 | tf_op jit(solution)/shard_map/all_to_all | solution.py:130
  321.2 25.3 %reduce.2 = f32[16,131072]{1,0:T(8,128)} reduce(f32[16,1,131072]{2,1,0:T(1,128)} %all-to-all-done, f32[]{:T(128)} %broadcast.140), dimensions={1}, to_apply=%all_to_all.24.reduce_sub_computation | reduce | bytes 16777220 | tf_op jit(solution)/shard_map/all_to_all | solution.py:130
  346.5 26.7 %reshape.133 = f32[8192,8,32]{2,1,0:T(8,128)} reshape(f32[16,131072]{1,0:T(8,128)} %reduce.2) | data formatting | bytes 16777216
  373.2 21.7 %copy.54 = f32[8,16,32,512]{3,2,1,0:T(8,128)} copy(f32[8,16,32,512]{2,0,3,1:T(8,128)} %bitcast.98) | data formatting | bytes 16777216 | tf_op jit(solution)/shard_map/all_to_all | solution.py:130
  394.9 9.3 %copy.55 = f32[8,512,512]{1,2,0:T(8,128)} copy(f32[8,512,512]{2,1,0:T(8,128)} %bitcast.104) | data formatting | bytes 16777216 | tf_op jit(solution)/shard_map/all_to_all | solution.py:130
  404.2 2.8 gather_fusion
  407.7 2.0 multiply_reduce_fusion
  412.5 1.9 fusion.42
  418.1 2.1 fusion.57
  420.1 1.9 select_subtract_fusion.5
  422.0 1.9 fusion.58
  423.9 1.9 fusion.59
  427.6 1.9 fusion.60
  429.5 1.9 fusion.61
  431.3 2.3 select_subtract_fusion.3
  439.2 1.9 fusion.64
  444.8 2.0 fusion.66
  448.7 18.0 %copy.60 = f32[8,32,16,512]{3,2,1,0:T(8,128)} copy(f32[8,32,16,512]{1,0,3,2:T(8,128)} %bitcast.99) | data formatting | bytes 16777216 | tf_op jit(solution)/shard_map/all_to_all | solution.py:130
  466.7 4.2 bitcast_reduce_fusion
  477.1 21.1 %add_bitcast_fusion = f32[8,512,512]{2,1,0:T(8,128)S(1)} fusion(f32[8,512]{1,0:T(8,128)S(1)} %broadcast_multiply_fusion, f32[8,512,512]{2,1,0:T(8,128)} %bitcast.105, f32[512,512]{1,0:T(8,128)S(1)} %fusion.68, f32[512]{0:T(512)S(1)} %broadcast_divide_fusion.3, f32[]{:T(128)S(6)} %sqrt.7), kind=kOutput, calls=%fused_computation.48 | convolution fusion | flops 12889620480 | bytes 17844228 | tf_op jit(solution)/shard_map/fjc,jk->fkc/dot_general | solution.py:95
  498.2 4.9 copy.57
  503.1 102.4 %all_to_all.33 = f32[8,512,512]{2,0,1:T(8,128)S(1)} all-to-all(f32[8,512,512]{2,0,1:T(8,128)S(1)} %copy.57), channel_id=1, replica_groups=mesh['gx'=2,'gy'=4,'mem'=16] {'mem'}, dimensions={1} | all-to-all | bytes 16777216 | tf_op jit(solution)/shard_map/all_to_all | solution.py:136
  605.5 8.1 %copy.58 = f32[8,32,16,512]{3,2,1,0:T(8,128)} copy(f32[8,32,16,512]{3,0,1,2:T(8,128)S(1)} %bitcast.106) | data formatting | bytes 16777216 | tf_op jit(solution)/shard_map/all_to_all | solution.py:136
  613.6 8.9 %reshape.118 = f32[8,32,64,128]{3,2,1,0:T(8,128)} reshape(f32[8,32,16,512]{3,2,1,0:T(8,128)} %copy.58) | data formatting | bytes 16777216 | tf_op jit(solution)/shard_map/reshape | solution.py:137
  (72 shorter events, 35.8 us)
Async XLA Ops:
  0.0 207.7 %copy-start = (s32[16,1]{0,1:T(1,128)S(1)}, s32[16,1]{0,1:T(1,128)}, u32[]{:S(2)}) copy-start(s32[16,1]{0,1:T(1,128)} %param.19) | copy-start | bytes 196
  1.8 6.4 %collective-permute-start.1 = (f32[256,1,128]{2,1,0:T(1,128)S(1)}, f32[256,1,128]{2,1,0:T(1,128)S(1)}, u32[]{:S(2)}, u32[]{:S(2)}) collective-permute-start(f32[256,1,128]{2,1,0:T(1,128)S(1)} %get-tuple-element.14), channel_id=1, source_target_pairs={{64,0},{0,64},{65,1},{1,65},{66,2},{2,66},{67,3},{3,67},{68,4},{4,... | collective-permute-start | bytes 393224 | tf_op jit(solution)/shard_map/ppermute | solution.py:20
  3.8 6.3 %collective-permute-start = (f32[256,1,128]{2,1,0:T(1,128)S(1)}, f32[256,1,128]{2,1,0:T(1,128)S(1)}, u32[]{:S(2)}, u32[]{:S(2)}) collective-permute-start(f32[256,1,128]{2,1,0:T(1,128)S(1)} %get-tuple-element.13), channel_id=1, source_target_pairs={{0,64},{64,0},{1,65},{65,1},{2,66},{66,2},{3,67},{67,3},{4,68},{68... | collective-permute-start | bytes 393224 | tf_op jit(solution)/shard_map/ppermute | solution.py:18
  22.0 15.5 %copy-start.15 = (f32[64,128]{1,0:T(8,128)S(1)}, f32[64,128]{1,0:T(8,128)}, u32[]{:S(2)}) copy-start(f32[64,128]{1,0:T(8,128)} %param.12) | copy-start | bytes 98308
  22.0 15.5 %copy-start.16 = (f32[64,128]{1,0:T(8,128)S(1)}, f32[64,128]{1,0:T(8,128)}, u32[]{:S(2)}) copy-start(f32[64,128]{1,0:T(8,128)} %param.11) | copy-start | bytes 98308
  28.1 9.5 %collective-permute-start.3 = (f32[256,66,1]{0,2,1:T(1,128)S(1)}, f32[256,66,1]{0,2,1:T(1,128)S(1)}, u32[]{:S(2)}, u32[]{:S(2)}) collective-permute-start(f32[256,66,1]{0,2,1:T(1,128)S(1)} %copy.46), channel_id=1, source_target_pairs={{16,0},{32,16},{48,32},{0,48},{17,1},{33,17},{49,33},{1,49},{18,2}... | collective-permute-start | bytes 202760 | tf_op jit(solution)/shard_map/ppermute | solution.py:20
  35.1 8.2 %collective-permute-start.2 = (f32[256,66,1]{0,2,1:T(1,128)S(1)}, f32[256,66,1]{0,2,1:T(1,128)S(1)}, u32[]{:S(2)}, u32[]{:S(2)}) collective-permute-start(f32[256,66,1]{0,2,1:T(1,128)S(1)} %copy.44), channel_id=1, source_target_pairs={{0,16},{16,32},{32,48},{48,0},{1,17},{17,33},{33,49},{49,1},{2,18}... | collective-permute-start | bytes 202760 | tf_op jit(solution)/shard_map/ppermute | solution.py:18
  37.6 11.4 %copy-start.5 = (f32[64,128]{1,0:T(8,128)}, f32[64,128]{1,0:T(8,128)S(1)}, u32[]{:S(2)}) copy-start(f32[64,128]{1,0:T(8,128)S(1)} %get-tuple-element.17) | copy-start | bytes 98308
  37.6 11.4 %copy-start.7 = (f32[64,128]{1,0:T(8,128)}, f32[64,128]{1,0:T(8,128)S(1)}, u32[]{:S(2)}) copy-start(f32[64,128]{1,0:T(8,128)S(1)} %get-tuple-element.18) | copy-start | bytes 98308
  37.6 11.4 %copy-start.9 = (f32[64,128]{1,0:T(8,128)}, f32[64,128]{1,0:T(8,128)S(1)}, u32[]{:S(2)}) copy-start(f32[64,128]{1,0:T(8,128)S(1)} %get-tuple-element.22) | copy-start | bytes 98308
  37.6 11.4 %copy-start.11 = (f32[64,128]{1,0:T(8,128)}, f32[64,128]{1,0:T(8,128)S(1)}, u32[]{:S(2)}) copy-start(f32[64,128]{1,0:T(8,128)S(1)} %get-tuple-element.23) | copy-start | bytes 98308
  37.6 11.4 %copy-start.13 = (f32[64,128]{1,0:T(8,128)S(1)}, f32[64,128]{1,0:T(8,128)}, u32[]{:S(2)}) copy-start(f32[64,128]{1,0:T(8,128)} %param.13) | copy-start | bytes 98308
  74.5 9.6 %copy-start.2 = (f32[256,64,128]{2,1,0:T(8,128)}, f32[256,64,128]{2,1,0:T(8,128)S(1)}, u32[]{:S(2)}) copy-start(f32[256,64,128]{2,1,0:T(8,128)S(1)} %fusion.20) | copy-start | bytes 25165828
  74.7 5.5 collective-permute-start.5
  76.5 5.3 collective-permute-start.4
  80.2 0.7 copy-start.3
  98.1 9.5 %collective-permute-start.7 = (f32[256,66,1]{0,2,1:T(1,128)S(1)}, f32[256,66,1]{0,2,1:T(1,128)S(1)}, u32[]{:S(2)}, u32[]{:S(2)}) collective-permute-start(f32[256,66,1]{0,2,1:T(1,128)S(1)} %copy.50), channel_id=1, source_target_pairs={{16,0},{32,16},{48,32},{0,48},{17,1},{33,17},{49,33},{1,49},{18,2}... | collective-permute-start | bytes 202760 | tf_op jit(solution)/shard_map/ppermute | solution.py:20
  104.3 14.7 %copy-start.4 = (f32[256,1,128]{2,1,0:T(1,128)S(1)}, f32[256,1,128]{2,1,0:T(1,128)}, u32[]{:S(2)}) copy-start(f32[256,1,128]{2,1,0:T(1,128)} %copy-done.3) | copy-start | bytes 393220
  104.3 14.7 %copy-start.6 = (f32[64,128]{1,0:T(8,128)S(1)}, f32[64,128]{1,0:T(8,128)}, u32[]{:S(2)}) copy-start(f32[64,128]{1,0:T(8,128)} %copy-done.5) | copy-start | bytes 98308
  104.3 14.7 %copy-start.8 = (f32[64,128]{1,0:T(8,128)S(1)}, f32[64,128]{1,0:T(8,128)}, u32[]{:S(2)}) copy-start(f32[64,128]{1,0:T(8,128)} %copy-done.7) | copy-start | bytes 98308
  104.3 14.7 %copy-start.10 = (f32[64,128]{1,0:T(8,128)S(1)}, f32[64,128]{1,0:T(8,128)}, u32[]{:S(2)}) copy-start(f32[64,128]{1,0:T(8,128)} %copy-done.9) | copy-start | bytes 98308
  104.3 14.7 %copy-start.12 = (f32[64,128]{1,0:T(8,128)S(1)}, f32[64,128]{1,0:T(8,128)}, u32[]{:S(2)}) copy-start(f32[64,128]{1,0:T(8,128)} %copy-done.11) | copy-start | bytes 98308
  104.3 14.7 %copy-start.14 = (f32[64,128]{1,0:T(8,128)S(1)}, f32[64,128]{1,0:T(8,128)}, u32[]{:S(2)}) copy-start(f32[64,128]{1,0:T(8,128)} %param.13) | copy-start | bytes 98308
  104.3 8.9 %collective-permute-start.6 = (f32[256,66,1]{0,2,1:T(1,128)S(1)}, f32[256,66,1]{0,2,1:T(1,128)S(1)}, u32[]{:S(2)}, u32[]{:S(2)}) collective-permute-start(f32[256,66,1]{0,2,1:T(1,128)S(1)} %copy.48), channel_id=1, source_target_pairs={{0,16},{16,32},{32,48},{48,0},{1,17},{17,33},{33,49},{49,1},{2,18}... | collective-permute-start | bytes 202760 | tf_op jit(solution)/shard_map/ppermute | solution.py:18
  199.6 121.1 %all-to-all-start = ((f32[16,1,131072]{2,1,0:T(1,128)}), f32[16,1,131072]{2,1,0:T(1,128)}, u32[]{:S(2)}, u32[]{:S(2)}) async-start(f32[16,1,131072]{2,1,0:T(1,128)} %reshape.132), calls=%async_computation | async-start | bytes 16777216 | tf_op jit(solution)/shard_map/all_to_all | solution.py:130
  605.5 17.1 %copy-start.1 = (s32[16,1]{0,1:T(1,128)S(1)}, s32[16,1]{0,1:T(1,128)}, u32[]{:S(2)}) copy-start(s32[16,1]{0,1:T(1,128)} %param.19) | copy-start | bytes 196
where the time goes:
time: 633 us; the launch traced here: 623 us
  local copies, waits for them, and re-layouts  221 us (35%)
  waiting for transfers between devices  121 us (19%)
  blocking collectives  102 us (16%)
  other arithmetic  90.7 us (14%)
  matrix products  67.4 us (11%)
  starting transfers between devices  19.2 us (3%)
    all_to_all x1, waiting for transfers between devices, on_device(): lax.all_to_all(stepped, 'mem', split_axis=2, concat_axis=1, tiled=True)  110 us
    all_to_all x1, blocking collectives, on_device(): lax.all_to_all(analysed, 'mem', split_axis=1, concat_axis=2, tiled=True)  102 us
    add x2, other arithmetic, update(): moved + spread * (eastern + western + northern + southern - 4.0 * centre)  52.7 us
    unnamed x36, local copies, waits for them, and re-layouts  51.6 us
    all_to_all x4, local copies, waits for them, and re-layouts, on_device(): lax.all_to_all(stepped, 'mem', split_axis=2, concat_axis=1, tiled=True)  49.5 us
    slice x6, local copies, waits for them, and re-layouts, with_halo(): lax.slice_in_dim(cells, cells.shape[dim] - width, cells.shape[dim], axis=...  29.9 us
    reshape x2, local copies, waits for them, and re-layouts, on_device(): stepped = stacked_fields.reshape(fields_all, members_dev, cells_x * cells_y)  29.2 us
    all_to_all x1, other arithmetic, on_device(): lax.all_to_all(stepped, 'mem', split_axis=2, concat_axis=1, tiled=True)  25.3 us
  transfers between devices with their start and end apart: 9, of which 5 were waited for; matrix products, arithmetic and copies ran while one was open for 4% of the time, Pallas kernels for 0%

commit v1 on v0

--- a/solution.py
+++ b/solution.py
@@ -133,7 +133,10 @@
     mixing = mixing_matrix(raw_values, own_value[0], own_precision[0], own_class[0], own_count[0])
     results[0].append(transform(groups[0], mixing))
     analysed = jnp.concatenate([pieces[0] for pieces in results], axis=0)
-    returned = lax.all_to_all(analysed, "mem", split_axis=1, concat_axis=2, tiled=True)
+    returned = jnp.concatenate(
+        lax.all_to_all(jnp.stack(jnp.split(analysed, lax.axis_size("mem"), axis=1)), "mem", 0, 0),
+        axis=2,
+    )
     return returned.reshape(fields_all, members_dev, cells_x, cells_y)
 
 

time: 633 us -> 628 us (level)
    another operation x0 -> x2, local copies, waits for them, and re-layouts: none -> 8.98 us  [the longest x1 8.94 us: on_device(): return returned.reshape(fields_all, members_dev, cells_x, cells_y)]
    all_to_all x1 -> x0, local copies, waits for them, and re-layouts: 8.11 us -> none  [on_device(): lax.all_to_all(analysed, 'mem', split_axis=1, concat_axis=2, tiled=True)]
    unnamed x36 -> x51, local copies, waits for them, and re-layouts: 51.6 us -> 52.1 us
where the time goes in v1:
time: 628 us; the launch traced here: 618 us
  local copies, waits for them, and re-layouts  217 us (35%)
  waiting for transfers between devices  121 us (19%)
  blocking collectives  103 us (16%)
  other arithmetic  90.7 us (14%)
  matrix products  67.1 us (11%)
  starting transfers between devices  19 us (3%)
    all_to_all x1, waiting for transfers between devices, on_device(): lax.all_to_all(stepped, 'mem', split_axis=2, concat_axis=1, tiled=True)  110 us
    all_to_all x1, blocking collectives, on_device(): lax.all_to_all(jnp.stack(jnp.split(analysed, lax.axis_size('mem'), axis=1...  103 us
    add x2, other arithmetic, update(): moved + spread * (eastern + western + northern + southern - 4.0 * centre)  52.7 us
    unnamed x51, local copies, waits for them, and re-layouts  52.1 us
    all_to_all x4, local copies, waits for them, and re-layouts, on_device(): lax.all_to_all(stepped, 'mem', split_axis=2, concat_axis=1, tiled=True)  49.7 us
    slice x6, local copies, waits for them, and re-layouts, with_halo(): lax.slice_in_dim(cells, cells.shape[dim] - width, cells.shape[dim], axis=...  29.9 us
    reshape x2, local copies, waits for them, and re-layouts, on_device(): stepped = stacked_fields.reshape(fields_all, members_dev, cells_x * cells_y)  29.2 us
    all_to_all x1, other arithmetic, on_device(): lax.all_to_all(stepped, 'mem', split_axis=2, concat_axis=1, tiled=True)  25.3 us
  transfers between devices with their start and end apart: 9, of which 5 were waited for; matrix products, arithmetic and copies ran while one was open for 4% of the time, Pallas kernels for 0%

profile of v1, /device:TPU:6, one launch (start us, length us, event | category | flops | bytes accessed | tf_op | source)
XLA Modules:
  0.0 618.5 jit_solution(72672091469546463)
XLA Ops:
  1.8 2.0 collective-permute-start.1
  3.9 4.3 collective-permute-done.1
  8.2 1.9 collective-permute-done
  10.1 4.1 pad_maximum_fusion
  14.1 7.9 %fusion.69 = (f32[256,66,1]{2,1,0:T(8,128)}, f32[256,66,1]{2,1,0:T(8,128)}) fusion(f32[256,66,128]{2,1,0:T(8,128)S(1)} %pad_maximum_fusion), kind=kLoop, calls=%fused_computation.144 | loop fusion | bytes 270336 | tf_op jit(solution)/shard_map/slice | solution.py:15
  22.0 6.1 copy.43
  29.0 6.1 copy.41
  35.1 2.5 collective-permute-start.2
  37.6 5.7 copy.44
  43.3 5.7 copy.42
  49.0 25.4 %fusion.20 = f32[256,64,128]{2,1,0:T(8,128)S(1)} fusion(f32[256,1,128]{2,1,0:T(1,128)S(1)} %collective-permute-done.1, f32[256,64,128]{2,1,0:T(8,128)} %bitcast.165, f32[256,1,128]{2,1,0:T(1,128)S(1)} %collective-permute-done, f32[256,66,1]{2,1,0:T(8,128)} %copy.44, f32[256,66,1]{2,1,0:T(8,128)} %copy.42, f32[64,128]{1,0:T(8,128)S(1)} %copy-done.13, ...), kind=kLoop, calls=%fused_computation.38 | loop fusion | flops 56623104 | bytes 17338368 | tf_op jit(solution)/shard_map/add | solution.py:30
  77.0 3.2 collective-permute-done.5
  81.7 2.3 pad_maximum_fusion.1
  84.1 7.9 %fusion.68 = (f32[256,66,1]{2,1,0:T(8,128)}, f32[256,66,1]{2,1,0:T(8,128)}) fusion(f32[256,66,128]{2,1,0:T(8,128)S(1)} %pad_maximum_fusion.1), kind=kLoop, calls=%fused_computation.143 | loop fusion | bytes 270336 | tf_op jit(solution)/shard_map/slice | solution.py:15
  92.0 6.1 copy.47
  98.1 6.1 copy.45
  104.3 3.3 collective-permute-start.6
  107.6 5.7 copy.48
  113.2 5.7 copy.46
  119.0 27.2 %fusion.6 = f32[256,64,128]{2,1,0:T(8,128)} fusion(f32[256,1,128]{2,1,0:T(1,128)S(1)} %copy-done.4, f32[256,64,128]{2,1,0:T(8,128)} %copy-done.2, f32[256,1,128]{2,1,0:T(1,128)} %collective-permute-done.4, f32[256,66,1]{2,1,0:T(8,128)} %copy.48, f32[256,66,1]{2,1,0:T(8,128)} %copy.46, f32[64,128]{1,0:T(8,128)S(1)} %copy-done.14, f32[64,128]{1,0:T(8,128)S(1)} %copy-done.8, ...), kind=kLoop, calls=%fused_computation.16 | loop fusion | flops 56623104 | bytes 17338368 | tf_op jit(solution)/shard_map/add | solution.py:30
  146.2 9.4 %reshape.116 = f32[8,32,8192]{2,1,0:T(8,128)} reshape(f32[256,64,128]{2,1,0:T(8,128)} %fusion.6) | data formatting | bytes 16777216 | tf_op jit(solution)/shard_map/reshape | solution.py:121
  155.6 19.8 %copy.49 = f32[8,32,8192]{1,0,2:T(8,128)} copy(f32[8,32,8192]{2,1,0:T(8,128)} %reshape.116) | data formatting | bytes 16777216 | tf_op jit(solution)/shard_map/reshape | solution.py:121
  175.4 24.2 %reshape.131 = f32[16,1,131072]{2,1,0:T(1,128)} reshape(f32[8192,8,32]{2,1,0:T(8,128)} %bitcast.162) | data formatting | bytes 16777216
  199.6 7.9 %all-to-all-start = ((f32[16,1,131072]{2,1,0:T(1,128)}), f32[16,1,131072]{2,1,0:T(1,128)}, u32[]{:S(2)}, u32[]{:S(2)}) async-start(f32[16,1,131072]{2,1,0:T(1,128)} %reshape.131), calls=%async_computation | async-start | bytes 16777216 | tf_op jit(solution)/shard_map/all_to_all | solution.py:130
  210.1 110.3 %all-to-all-done = f32[16,1,131072]{2,1,0:T(1,128)} async-done(((f32[16,1,131072]{2,1,0:T(1,128)}), f32[16,1,131072]{2,1,0:T(1,128)}, u32[]{:S(2)}, u32[]{:S(2)}) %all-to-all-start) | async-done | bytes 8388640 | tf_op jit(solution)/shard_map/all_to_all | solution.py:130
  321.0 25.3 %reduce.2 = f32[16,131072]{1,0:T(8,128)} reduce(f32[16,1,131072]{2,1,0:T(1,128)} %all-to-all-done, f32[]{:T(128)} %broadcast.140), dimensions={1}, to_apply=%all_to_all.16.reduce_sub_computation | reduce | bytes 16777220 | tf_op jit(solution)/shard_map/all_to_all | solution.py:130
  346.3 26.7 %reshape.132 = f32[8192,8,32]{2,1,0:T(8,128)} reshape(f32[16,131072]{1,0:T(8,128)} %reduce.2) | data formatting | bytes 16777216
  373.0 21.7 %copy.51 = f32[8,16,32,512]{3,2,1,0:T(8,128)} copy(f32[8,16,32,512]{2,0,3,1:T(8,128)} %bitcast.160) | data formatting | bytes 16777216 | tf_op jit(solution)/shard_map/all_to_all | solution.py:130
  394.7 9.5 %copy.52 = f32[8,512,512]{1,2,0:T(8,128)} copy(f32[8,512,512]{2,1,0:T(8,128)} %bitcast.166) | data formatting | bytes 16777216 | tf_op jit(solution)/shard_map/all_to_all | solution.py:130
  404.2 2.8 gather_fusion
  407.7 2.0 multiply_reduce_fusion
  412.5 1.9 fusion.58
  418.1 2.0 fusion.73
  422.0 1.9 fusion.74
  427.6 1.9 fusion.76
  429.4 1.9 fusion.77
  431.3 2.1 select_subtract_fusion.3
  433.4 1.9 fusion.78
  435.2 1.9 fusion.79
  439.0 1.9 fusion.80
  440.8 1.9 fusion.81
  444.6 2.3 fusion.82
  448.7 18.0 %copy.56 = f32[8,32,16,512]{3,2,1,0:T(8,128)} copy(f32[8,32,16,512]{1,0,3,2:T(8,128)} %bitcast.161) | data formatting | bytes 16777216 | tf_op jit(solution)/shard_map/all_to_all | solution.py:130
  466.7 4.2 bitcast_reduce_fusion
  477.1 20.8 %add_bitcast_fusion = f32[8,512,512]{2,1,0:T(8,128)S(1)} fusion(f32[8,512]{1,0:T(8,128)S(1)} %broadcast_multiply_fusion, f32[8,512,512]{2,1,0:T(8,128)} %bitcast.167, f32[512,512]{1,0:T(8,128)S(1)} %fusion.84, f32[512]{0:T(512)S(1)} %broadcast_divide_fusion.3, f32[]{:T(128)S(6)} %sqrt.7), kind=kOutput, calls=%fused_computation.48 | convolution fusion | flops 12889620480 | bytes 17844228 | tf_op jit(solution)/shard_map/fjc,jk->fkc/dot_general | solution.py:95
  498.7 102.6 %all_to_all.23 = f32[16,8,32,512]{3,2,1,0:T(8,128)S(1)} all-to-all(f32[16,8,32,512]{3,2,1,0:T(8,128)S(1)} %fusion.37), channel_id=1, replica_groups=mesh['gx'=2,'gy'=4,'mem'=16] {'mem'}, dimensions={0} | all-to-all | bytes 16777216 | tf_op jit(solution)/shard_map/all_to_all | solution.py:137
  601.3 8.0 %copy.54 = f32[8,32,16,512]{3,2,1,0:T(8,128)} copy(f32[8,32,16,512]{3,1,0,2:T(8,128)S(1)} %bitcast.168) | data formatting | bytes 16777216 | tf_op jit(solution)/shard_map/reshape | solution.py:136
  609.3 8.9 %reshape_reshape.3 = f32[8,32,64,128]{3,2,1,0:T(8,128)} reshape(f32[8,32,16,512]{3,2,1,0:T(8,128)} %copy.54) | data formatting | bytes 16777216 | tf_op jit(solution)/shard_map/reshape;reshape | solution.py:140
  (87 shorter events, 34.5 us)
Async XLA Ops:
  0.0 207.4 %copy-start = (s32[16,1]{0,1:T(1,128)S(1)}, s32[16,1]{0,1:T(1,128)}, u32[]{:S(2)}) copy-start(s32[16,1]{0,1:T(1,128)} %param.19) | copy-start | bytes 196
  1.8 6.4 %collective-permute-start.1 = (f32[256,1,128]{2,1,0:T(1,128)S(1)}, f32[256,1,128]{2,1,0:T(1,128)S(1)}, u32[]{:S(2)}, u32[]{:S(2)}) collective-permute-start(f32[256,1,128]{2,1,0:T(1,128)S(1)} %get-tuple-element.14), channel_id=1, source_target_pairs={{64,0},{0,64},{65,1},{1,65},{66,2},{2,66},{67,3},{3,67},{68,4},{4,... | collective-permute-start | bytes 393224 | tf_op jit(solution)/shard_map/ppermute | solution.py:20
  3.8 6.3 %collective-permute-start = (f32[256,1,128]{2,1,0:T(1,128)S(1)}, f32[256,1,128]{2,1,0:T(1,128)S(1)}, u32[]{:S(2)}, u32[]{:S(2)}) collective-permute-start(f32[256,1,128]{2,1,0:T(1,128)S(1)} %get-tuple-element.13), channel_id=1, source_target_pairs={{0,64},{64,0},{1,65},{65,1},{2,66},{66,2},{3,67},{67,3},{4,68},{68... | collective-permute-start | bytes 393224 | tf_op jit(solution)/shard_map/ppermute | solution.py:18
  22.0 15.5 %copy-start.15 = (f32[64,128]{1,0:T(8,128)S(1)}, f32[64,128]{1,0:T(8,128)}, u32[]{:S(2)}) copy-start(f32[64,128]{1,0:T(8,128)} %param.12) | copy-start | bytes 98308
  22.0 15.5 %copy-start.16 = (f32[64,128]{1,0:T(8,128)S(1)}, f32[64,128]{1,0:T(8,128)}, u32[]{:S(2)}) copy-start(f32[64,128]{1,0:T(8,128)} %param.11) | copy-start | bytes 98308
  28.1 9.5 %collective-permute-start.3 = (f32[256,66,1]{0,2,1:T(1,128)S(1)}, f32[256,66,1]{0,2,1:T(1,128)S(1)}, u32[]{:S(2)}, u32[]{:S(2)}) collective-permute-start(f32[256,66,1]{0,2,1:T(1,128)S(1)} %copy.43), channel_id=1, source_target_pairs={{16,0},{32,16},{48,32},{0,48},{17,1},{33,17},{49,33},{1,49},{18,2}... | collective-permute-start | bytes 202760 | tf_op jit(solution)/shard_map/ppermute | solution.py:20
  35.1 8.2 %collective-permute-start.2 = (f32[256,66,1]{0,2,1:T(1,128)S(1)}, f32[256,66,1]{0,2,1:T(1,128)S(1)}, u32[]{:S(2)}, u32[]{:S(2)}) collective-permute-start(f32[256,66,1]{0,2,1:T(1,128)S(1)} %copy.41), channel_id=1, source_target_pairs={{0,16},{16,32},{32,48},{48,0},{1,17},{17,33},{33,49},{49,1},{2,18}... | collective-permute-start | bytes 202760 | tf_op jit(solution)/shard_map/ppermute | solution.py:18
  37.6 11.4 %copy-start.5 = (f32[64,128]{1,0:T(8,128)}, f32[64,128]{1,0:T(8,128)S(1)}, u32[]{:S(2)}) copy-start(f32[64,128]{1,0:T(8,128)S(1)} %get-tuple-element.17) | copy-start | bytes 98308
  37.6 11.4 %copy-start.7 = (f32[64,128]{1,0:T(8,128)}, f32[64,128]{1,0:T(8,128)S(1)}, u32[]{:S(2)}) copy-start(f32[64,128]{1,0:T(8,128)S(1)} %get-tuple-element.18) | copy-start | bytes 98308
  37.6 11.4 %copy-start.9 = (f32[64,128]{1,0:T(8,128)}, f32[64,128]{1,0:T(8,128)S(1)}, u32[]{:S(2)}) copy-start(f32[64,128]{1,0:T(8,128)S(1)} %get-tuple-element.22) | copy-start | bytes 98308
  37.6 11.4 %copy-start.11 = (f32[64,128]{1,0:T(8,128)}, f32[64,128]{1,0:T(8,128)S(1)}, u32[]{:S(2)}) copy-start(f32[64,128]{1,0:T(8,128)S(1)} %get-tuple-element.23) | copy-start | bytes 98308
  37.6 11.4 %copy-start.13 = (f32[64,128]{1,0:T(8,128)S(1)}, f32[64,128]{1,0:T(8,128)}, u32[]{:S(2)}) copy-start(f32[64,128]{1,0:T(8,128)} %param.13) | copy-start | bytes 98308
  74.5 9.6 %copy-start.2 = (f32[256,64,128]{2,1,0:T(8,128)}, f32[256,64,128]{2,1,0:T(8,128)S(1)}, u32[]{:S(2)}) copy-start(f32[256,64,128]{2,1,0:T(8,128)S(1)} %fusion.20) | copy-start | bytes 25165828
  74.7 5.5 collective-permute-start.5
  76.5 5.2 collective-permute-start.4
  80.2 0.7 copy-start.3
  98.1 9.5 %collective-permute-start.7 = (f32[256,66,1]{0,2,1:T(1,128)S(1)}, f32[256,66,1]{0,2,1:T(1,128)S(1)}, u32[]{:S(2)}, u32[]{:S(2)}) collective-permute-start(f32[256,66,1]{0,2,1:T(1,128)S(1)} %copy.47), channel_id=1, source_target_pairs={{16,0},{32,16},{48,32},{0,48},{17,1},{33,17},{49,33},{1,49},{18,2}... | collective-permute-start | bytes 202760 | tf_op jit(solution)/shard_map/ppermute | solution.py:20
  104.2 14.7 %copy-start.4 = (f32[256,1,128]{2,1,0:T(1,128)S(1)}, f32[256,1,128]{2,1,0:T(1,128)}, u32[]{:S(2)}) copy-start(f32[256,1,128]{2,1,0:T(1,128)} %copy-done.3) | copy-start | bytes 393220
  104.2 14.7 %copy-start.6 = (f32[64,128]{1,0:T(8,128)S(1)}, f32[64,128]{1,0:T(8,128)}, u32[]{:S(2)}) copy-start(f32[64,128]{1,0:T(8,128)} %copy-done.5) | copy-start | bytes 98308
  104.3 14.7 %copy-start.8 = (f32[64,128]{1,0:T(8,128)S(1)}, f32[64,128]{1,0:T(8,128)}, u32[]{:S(2)}) copy-start(f32[64,128]{1,0:T(8,128)} %copy-done.7) | copy-start | bytes 98308
  104.3 14.7 %copy-start.10 = (f32[64,128]{1,0:T(8,128)S(1)}, f32[64,128]{1,0:T(8,128)}, u32[]{:S(2)}) copy-start(f32[64,128]{1,0:T(8,128)} %copy-done.9) | copy-start | bytes 98308
  104.3 14.7 %copy-start.12 = (f32[64,128]{1,0:T(8,128)S(1)}, f32[64,128]{1,0:T(8,128)}, u32[]{:S(2)}) copy-start(f32[64,128]{1,0:T(8,128)} %copy-done.11) | copy-start | bytes 98308
  104.3 14.7 %copy-start.14 = (f32[64,128]{1,0:T(8,128)S(1)}, f32[64,128]{1,0:T(8,128)}, u32[]{:S(2)}) copy-start(f32[64,128]{1,0:T(8,128)} %param.13) | copy-start | bytes 98308
  104.3 8.9 %collective-permute-start.6 = (f32[256,66,1]{0,2,1:T(1,128)S(1)}, f32[256,66,1]{0,2,1:T(1,128)S(1)}, u32[]{:S(2)}, u32[]{:S(2)}) collective-permute-start(f32[256,66,1]{0,2,1:T(1,128)S(1)} %copy.45), channel_id=1, source_target_pairs={{0,16},{16,32},{32,48},{48,0},{1,17},{17,33},{33,49},{49,1},{2,18}... | collective-permute-start | bytes 202760 | tf_op jit(solution)/shard_map/ppermute | solution.py:18
  199.6 120.9 %all-to-all-start = ((f32[16,1,131072]{2,1,0:T(1,128)}), f32[16,1,131072]{2,1,0:T(1,128)}, u32[]{:S(2)}, u32[]{:S(2)}) async-start(f32[16,1,131072]{2,1,0:T(1,128)} %reshape.131), calls=%async_computation | async-start | bytes 16777216 | tf_op jit(solution)/shard_map/all_to_all | solution.py:130
  601.3 16.9 %copy-start.1 = (s32[16,1]{0,1:T(1,128)S(1)}, s32[16,1]{0,1:T(1,128)}, u32[]{:S(2)}) copy-start(s32[16,1]{0,1:T(1,128)} %param.19) | copy-start | bytes 196
